TPU v7x, 32 devices: a whole 2x2x4 slice. The times are simulated.
32 devices in a mesh: wide: 8 (over y, x, core), narrow: 4 (over z).
Axes of the slice: x: 2, y: 2, z: 4, core: 2. Of those that a mesh axis runs over, the one named last changes fastest.
Arguments:
- tokens: bfloat16 [2048, 2048], P('wide', 'narrow'), may hold values from -6 to 6
- norm_gain: bfloat16 [2048], replicated, may hold values from 0.25 to 1.75
- router: bfloat16 [2048, 8], replicated, may hold values from -0.125 to 0.125
- routes: int32 [2048, 2], P('wide'), may hold values from 0 to 7, all different within a row
- kv_weight: bfloat16 [4096, 2048], P('narrow', 'wide'), may hold values from -0.125 to 0.125
- query_weight: bfloat16 [16384, 2048], P('narrow', 'wide'), may hold values from -0.125 to 0.125
- out_weight: bfloat16 [16384, 2048], P('narrow', 'wide'), may hold values from -0.09375 to 0.09375
- prefix_cache: bfloat16 [6144, 4096], P('wide', 'narrow'), may hold values from -225 to 225
- suffix_lengths: int32 [4], replicated, may hold values from 1 to 1280, 2048 in all
- prefix_lengths: int32 [4], replicated, may hold values from 1 to 3072, 6144 in all
Outputs:
- mixed: bfloat16 [2048, 2048], P('wide', 'narrow')
Inputs may be any that keep to these rules, and one draw needn't show every extreme that they name: `routes`: each token names 2 different experts. `suffix_lengths`: they sum to 2048. `prefix_lengths`: they sum to 6144.
All inputs are finite; a program needn't handle non-finite values.
Results may differ from a plain program's by a relative error of at most 0.012.
The roundings to bfloat16 on the way count: a program that leaves them out, or rounds other values in their place, can miss the bound.
Values may be sent and summed in bfloat16 or wider, within the bound.
A program may use at most 320 MiB of HBM per device.

v0:
```python
import functools
import math

import jax
import jax.numpy as jnp
from jax import lax
from jax.experimental import pallas as pl
from jax.experimental.pallas import tpu as pltpu
from jax.sharding import PartitionSpec as P

H = 128
E = 8
EPS = 1e-06
FLOOR = -1e30
F32 = jnp.float32
BF16 = jnp.bfloat16
NT = (((1,), (1,)), ((), ()))
TN = (((0,), (0,)), ((), ()))


def pick(routes_column, blocks):
    found = jnp.zeros_like(blocks[0])
    for expert, block in enumerate(blocks):
        found = jnp.where(routes_column == expert, block, found)
    return found


def route_columns(routes_rows):
    turned = jnp.transpose(routes_rows)
    return turned[:, 0:1], turned[:, 1:2]


def attend_kernel(
    group, suffix_ref, prefix_ref, sub_ref, queries_ref, gates_ref, cache_ref, kv_ref, out_ref
):
    strands, rows = queries_ref.shape[:2]
    for_each = functools.partial(
        attend_strand, group, strands, rows // 2, suffix_ref, prefix_ref, sub_ref, queries_ref,
        gates_ref, cache_ref, kv_ref, out_ref
    )
    lax.fori_loop(0, strands, lambda i, none: for_each(i), None)


def attend_strand(
    group, strands, block, suffix_ref, prefix_ref, sub_ref, queries_ref, gates_ref, cache_ref,
    kv_ref, out_ref, strand
):
    tenants = suffix_ref.shape[0]
    cache_block = math.gcd(cache_ref.shape[0], 512)
    token_block = strand * group + sub_ref[0]
    first = token_block * block
    last = first + block - 1
    queries = queries_ref[strand]

    token = first + lax.broadcasted_iota(jnp.int32, (1, block), 1)
    low = jnp.zeros((1, block), jnp.int32)
    high = jnp.zeros((1, block), jnp.int32)
    start = jnp.zeros((1, block), jnp.int32)
    low_first = high_first = start_first = jnp.int32(0)
    low_last = high_last = start_last = jnp.int32(0)
    suffix_at = prefix_at = jnp.int32(0)
    for tenant in range(tenants):
        suffix_end = suffix_at + suffix_ref[tenant]
        prefix_end = prefix_at + prefix_ref[tenant]
        inside = (token >= suffix_at) & (token < suffix_end)
        low = jnp.where(inside, prefix_at, low)
        high = jnp.where(inside, prefix_end, high)
        start = jnp.where(inside, suffix_at, start)
        holds_first = (first >= suffix_at) & (first < suffix_end)
        holds_last = (last >= suffix_at) & (last < suffix_end)
        low_first = jnp.where(holds_first, prefix_at, low_first)
        high_first = jnp.where(holds_first, prefix_end, high_first)
        start_first = jnp.where(holds_first, suffix_at, start_first)
        low_last = jnp.where(holds_last, prefix_at, low_last)
        high_last = jnp.where(holds_last, prefix_end, high_last)
        start_last = jnp.where(holds_last, suffix_at, start_last)
        suffix_at, prefix_at = suffix_end, prefix_end
    twice = lambda row: jnp.concatenate([row, row], axis=1)
    low, high, start, upto = twice(low), twice(high), twice(start), twice(token + 1)
    to_log2 = math.log2(math.e) * H ** (-0.5)
    rows = 2 * block

    def over(carried, here, limits):
        highest, totals, summed = carried
        scores = lax.dot_general(here[:, :H], queries, NT, preferred_element_type=F32)
        if limits is not None:
            key_first, row_low, row_high = limits
            at = lax.broadcasted_iota(jnp.int32, scores.shape, 0)
            scores = jnp.where(
                (at >= row_low - key_first) & (at < row_high - key_first), scores, -jnp.inf
            )
        new_highest = jnp.maximum(highest, jnp.max(scores, axis=0, keepdims=True))
        weights = jnp.exp2((scores - new_highest) * to_log2)
        factor = jnp.exp2((highest - new_highest) * to_log2)
        totals = totals * factor + jnp.sum(weights, axis=0, keepdims=True)
        summed = summed * factor + lax.dot_general(
            here[:, H:], weights.astype(BF16), TN, preferred_element_type=F32
        )
        return new_highest, totals, summed

    def cache_at(step):
        return cache_ref[pl.ds(pl.multiple_of(step * cache_block, cache_block), cache_block), :]

    def suffix_at_step(step):
        place = lax.rem(step, group) * strands + lax.div(step, group)
        return kv_ref[pl.ds(pl.multiple_of(place * block, block), block), :]

    def through(carried, begin, inner_begin, inner_end, end, load, limits_at):
        inner_begin = jnp.minimum(inner_begin, end)
        inner_end = jnp.maximum(inner_end, inner_begin)
        left = inner_begin - begin

        def masked(turn, carried):
            step = begin + turn + jnp.where(turn < left, 0, inner_end - inner_begin)
            return over(carried, load(step), limits_at(step))

        carried = lax.fori_loop(0, end - begin - (inner_end - inner_begin), masked, carried)
        return lax.fori_loop(
            inner_begin, inner_end, lambda step, now: over(now, load(step), None), carried
        )

    carried = (
        jnp.full((1, rows), FLOOR, F32),
        jnp.zeros((1, rows), F32),
        jnp.zeros((H, rows), F32),
    )
    carried = through(
        carried,
        lax.div(low_first, cache_block),
        lax.div(low_last + cache_block - 1, cache_block),
        lax.div(high_first, cache_block),
        lax.div(high_last + cache_block - 1, cache_block),
        cache_at,
        lambda step: (step * cache_block, low, high),
    )
    carried = through(
        carried,
        lax.div(start_first, block),
        lax.div(start_last + block - 1, block),
        token_block,
        token_block + 1,
        suffix_at_step,
        lambda step: (step * block, start, upto),
    )
    unused, totals, summed = carried
    attended = jnp.transpose(summed / totals) * gates_ref[strand]
    out_ref[strand, 0] = attended[:block].astype(BF16)
    out_ref[strand, 1] = attended[block:].astype(BF16)


def remote(source, target, send_sem, recv_sem, place):
    return pltpu.make_async_remote_copy(
        src_ref=source,
        dst_ref=target,
        send_sem=send_sem,
        recv_sem=recv_sem,
        device_id=place,
        device_id_type=pl.DeviceIdType.MESH,
    )


def greet(place):
    pl.semaphore_signal(
        pltpu.get_barrier_semaphore(),
        inc=1,
        device_id=place,
        device_id_type=pl.DeviceIdType.MESH,
    )


def prepare_kernel(
    wide, narrow, group, tokens_ref, gain_ref, routes_ref, router_ref, kvw_ref, query_ref,
    cache_ref, queries_out, gates_out, cache_out, kv_out, routes_out,
    held_tokens, normed_out, held_kvw, held_query, held_routes,
    tok_send, tok_recv, rt_send, rt_recv, first_send, first_recv, pass_send, pass_recv,
    sib_send, sib_recv, near_send, near_recv, kv_send, kv_recv, local_sem
):
    heads = wide // group
    block, features = tokens_ref.shape
    columns = kvw_ref.shape[1]
    slots = cache_ref.shape[0]
    me, depth = lax.axis_index("wide"), lax.axis_index("narrow")
    head, sub = lax.div(me, group), lax.rem(me, group)

    for k in range(1, wide):
        greet((lax.rem(me + k, wide), depth))
    for k in range(1, narrow):
        greet((me, lax.rem(depth + k, narrow)))
    pl.semaphore_wait(pltpu.get_barrier_semaphore(), wide - 1 + narrow - 1)

    def ahead(ka):
        return lax.rem(head + ka, heads)

    def behind(ka):
        return lax.rem(head + heads - ka, heads)

    def sibling(ks):
        return (head * group + lax.rem(sub + ks, group), depth)

    def sub_behind(s, ks):
        return lax.rem(s + group - ks, group)

    def source(kind, of_head, part):
        whole = (2 * H, E * H, slots)[kind]
        size = whole if part is None else whole // group
        offset = 0 if part is None else part * size
        if kind == 2:
            return cache_ref.at[
                pl.ds(pl.multiple_of(offset, 16), size),
                pl.ds(pl.multiple_of(of_head * 2 * H, 2 * H), 2 * H),
            ]
        ref = (kvw_ref, query_ref)[kind]
        return ref.at[pl.ds(pl.multiple_of(of_head * whole + offset, 16), size), :]

    def target(kind, origin, part):
        whole = (2 * H, E * H, slots)[kind]
        size = whole if part is None else whole // group
        offset = 0 if part is None else part * size
        if kind == 2:
            return cache_out.at[pl.ds(pl.multiple_of(origin * slots + offset, 16), size), :]
        ref = (held_kvw, held_query)[kind]
        return ref.at[
            pl.ds(pl.multiple_of(offset, 16), size),
            pl.ds(pl.multiple_of(origin * columns, columns), columns),
        ]

    def tok(k):
        return remote(
            tokens_ref, held_tokens.at[depth], tok_send.at[k], tok_recv.at[k],
            (me, lax.rem(depth + k, narrow))
        )

    def tok_in(k):
        return remote(
            tokens_ref, held_tokens.at[lax.rem(depth + narrow - k, narrow)], tok_send.at[k],
            tok_recv.at[k], (me, lax.rem(depth + k, narrow))
        )

    def rt(k):
        return remote(
            held_routes, routes_out.at[me], rt_send.at[k], rt_recv.at[k],
            (lax.rem(me + k, wide), depth)
        )

    def rt_in(k):
        return remote(
            held_routes, routes_out.at[lax.rem(me + wide - k, wide)], rt_send.at[k],
            rt_recv.at[k], (lax.rem(me + k, wide), depth)
        )

    def first(kind, ka, ks):
        to_sub = lax.rem(sub + ks, group)
        return remote(
            source(kind, ahead(ka), to_sub), target(kind, me, to_sub),
            first_send.at[kind, ka, ks], first_recv.at[kind, ka, ks],
            (ahead(ka) * group + to_sub, depth)
        )

    def first_in(kind, ka, ks):
        origin = behind(ka) * group + sub_behind(sub, ks)
        return remote(
            source(kind, head, sub), target(kind, origin, sub),
            first_send.at[kind, ka, ks], first_recv.at[kind, ka, ks], (origin, depth)
        )

    def hand(kind, ka, ks, js):
        held = target(kind, behind(ka) * group + sub_behind(sub, ks), sub)
        return remote(
            held, held, pass_send.at[kind, ka, ks, js], pass_recv.at[kind, ka, ks, js], sibling(js)
        )

    def hand_in(kind, ka, ks, js):
        other = sub_behind(sub, js)
        held = target(kind, behind(ka) * group + sub_behind(other, ks), other)
        return remote(
            held, held, pass_send.at[kind, ka, ks, js], pass_recv.at[kind, ka, ks, js], sibling(js)
        )

    def sib(kind, js):
        return remote(
            source(kind, head, None), target(kind, me, None), sib_send.at[kind, js],
            sib_recv.at[kind, js], sibling(js)
        )

    def sib_in(kind, js):
        return remote(
            source(kind, head, None), target(kind, head * group + sub_behind(sub, js), None),
            sib_send.at[kind, js], sib_recv.at[kind, js], sibling(js)
        )

    def local(kind):
        return pltpu.make_async_copy(
            source(kind, head, None), target(kind, me, None), local_sem.at[kind]
        )

    def launch(kind):
        for ka in range(1, heads):
            for ks in range(group):
                first(kind, ka, ks).start()
        for js in range(1, group):
            sib(kind, js).start()
        local(kind).start()

    def relay(kind):
        for ka in range(1, heads):
            for ks in range(group):
                first_in(kind, ka, ks).wait_recv()
                for js in range(1, group):
                    hand(kind, ka, ks, js).start()

    def settle(kind):
        local(kind).wait()
        for js in range(1, group):
            sib_in(kind, js).wait_recv()
            for ka in range(1, heads):
                for ks in range(group):
                    hand_in(kind, ka, ks, js).wait_recv()

    for k in range(1, narrow):
        tok(k).start()
    held_routes[...] = jnp.zeros_like(held_routes)
    held_routes[0:2, :] = routes_ref[...]
    for k in range(1, wide):
        rt(k).start()
    launch(0)
    launch(1)
    routes_out[me] = held_routes[...]
    held_tokens[depth] = tokens_ref[...]
    for k in range(1, narrow):
        tok_in(k).wait_recv()
    squares = jnp.zeros((block, 1), F32)
    for k in range(narrow):
        floats = held_tokens[k].astype(F32)
        squares = squares + jnp.sum(floats * floats, axis=1, keepdims=True)
    inverse = lax.rsqrt(squares / (narrow * features) + EPS)
    for k in range(narrow):
        at = slice(k * features, (k + 1) * features)
        normed_out[head, :, at] = (
            held_tokens[k].astype(F32) * inverse * gain_ref[at].astype(F32)[None, :]
        ).astype(BF16)

    square = heads == 4
    half = block // 2
    if square:
        x, y = lax.rem(head, 2), lax.div(head, 2)
        neighbour = [y * 2 + 1 - x, (1 - y) * 2 + x]
        far = (1 - y) * 2 + 1 - x

    def near(side, piece):
        held = normed_out.at[head, pl.ds(piece * half, half), :]
        return remote(
            held, held, near_send.at[side, piece], near_recv.at[side, piece],
            (neighbour[side] * group + sub, depth)
        )

    def near_in(side, piece):
        held = normed_out.at[neighbour[side], pl.ds(piece * half, half), :]
        return remote(
            held, held, near_send.at[side, piece], near_recv.at[side, piece],
            (neighbour[side] * group + sub, depth)
        )

    def onward(piece):
        held = normed_out.at[neighbour[piece], pl.ds(piece * half, half), :]
        return remote(
            held, held, near_send.at[2, piece], near_recv.at[2, piece],
            (neighbour[1 - piece] * group + sub, depth)
        )

    def onward_in(piece):
        held = normed_out.at[far, pl.ds(piece * half, half), :]
        return remote(
            held, held, near_send.at[2, piece], near_recv.at[2, piece],
            (neighbour[1 - piece] * group + sub, depth)
        )

    def straight(ka):
        held = normed_out.at[head]
        return remote(
            held, held, near_send.at[0, ka], near_recv.at[0, ka], (ahead(ka) * group + sub, depth)
        )

    def straight_in(ka):
        held = normed_out.at[behind(ka)]
        return remote(
            held, held, near_send.at[0, ka], near_recv.at[0, ka], (behind(ka) * group + sub, depth)
        )

    if square:
        for turn in range(2):
            for side in range(2):
                near(side, (side + turn) % 2).start()
    else:
        for ka in range(1, heads):
            straight(ka).start()
    launch(2)
    relay(0)
    settle(0)

    def keys_values(strand):
        total = lax.dot_general(
            normed_out[strand], held_kvw[...], NT, preferred_element_type=F32
        )
        kv_out[sub, strand] = total.astype(BF16)

    def queries_of(strand):
        normed = normed_out[strand]
        logits = lax.dot_general(normed, router_ref[...], NT, preferred_element_type=F32)
        expert_at = lax.broadcasted_iota(jnp.int32, logits.shape, 1)
        route_a, route_b = route_columns(routes_out[strand * group + sub])
        logit_a = jnp.sum(jnp.where(expert_at == route_a, logits, 0.0), axis=1, keepdims=True)
        logit_b = jnp.sum(jnp.where(expert_at == route_b, logits, 0.0), axis=1, keepdims=True)
        top = jnp.maximum(logit_a, logit_b)
        up_a, up_b = jnp.exp(logit_a - top), jnp.exp(logit_b - top)
        gates_out[strand, :block] = up_a / (up_a + up_b)
        gates_out[strand, block:] = up_b / (up_a + up_b)
        every = lax.dot_general(normed, held_query[...], NT, preferred_element_type=F32)
        parts = [every[:, e * H:(e + 1) * H] for e in range(E)]
        queries_out[strand, :block] = pick(route_a, parts).astype(BF16)
        queries_out[strand, block:] = pick(route_b, parts).astype(BF16)

    def kv_pair(k, strand, js):
        held = kv_out.at[sub, strand]
        return remote(held, held, kv_send.at[k, js], kv_recv.at[k, js], sibling(js))

    def kv_pair_in(k, strand, js):
        held = kv_out.at[sub_behind(sub, js), strand]
        return remote(held, held, kv_send.at[k, js], kv_recv.at[k, js], sibling(js))

    if square:
        order = [head, neighbour[0], neighbour[1], far]
    else:
        order = [behind(ka) for ka in range(heads)]

    def strand_done(k):
        keys_values(order[k])
        for js in range(1, group):
            kv_pair(k, order[k], js).start()

    strand_done(0)
    relay(1)
    if square:
        for piece in range(2):
            near_in(piece, piece).wait_recv()
            onward(piece).start()
        for side in range(2):
            near_in(side, 1 - side).wait_recv()
            strand_done(1 + side)
    else:
        for ka in range(1, heads):
            straight_in(ka).wait_recv()
            strand_done(ka)
    settle(1)
    for k in range(1, wide):
        rt_in(k).wait_recv()
    if square:
        def early(k, none):
            queries_of(jnp.where(k == 0, head, jnp.where(k == 1, neighbour[0], neighbour[1])))

        lax.fori_loop(0, 3, early, None)
    else:
        lax.fori_loop(0, heads, lambda k, none: queries_of(k), None)
    relay(2)
    if square:
        for piece in range(2):
            onward_in(piece).wait_recv()
        strand_done(3)
        queries_of(far)
    settle(2)
    for k in range(heads):
        for js in range(1, group):
            kv_pair_in(k, order[k], js).wait_recv()

    for k in range(1, narrow):
        tok(k).wait_send()
    for k in range(1, wide):
        rt(k).wait_send()
    for kind in range(3):
        for js in range(1, group):
            sib(kind, js).wait_send()
        for ka in range(1, heads):
            for ks in range(group):
                first(kind, ka, ks).wait_send()
                for js in range(1, group):
                    hand(kind, ka, ks, js).wait_send()
    if square:
        for side in range(2):
            for piece in range(2):
                near(side, piece).wait_send()
        for piece in range(2):
            onward(piece).wait_send()
    else:
        for ka in range(1, heads):
            straight(ka).wait_send()
    for k in range(heads):
        for js in range(1, group):
            kv_pair(k, order[k], js).wait_send()


def finish_kernel(
    wide, narrow, group, attended_ref, weight_ref, routes_ref, out_ref,
    gathered, parts, got, mine, final,
    ring_send, ring_recv, pair_send, pair_recv, pass_send, pass_recv,
    deep_send, deep_recv, turn_send, turn_recv
):
    heads = wide // group
    ratio = wide // narrow
    block = attended_ref.shape[2]
    columns = weight_ref.shape[1]
    me, depth = lax.axis_index("wide"), lax.axis_index("narrow")
    head, sub = lax.div(me, group), lax.rem(me, group)
    turned = lax.div(me, ratio)
    lane = lax.rem(me, ratio)

    for k in range(1, wide):
        greet((lax.rem(me + k, wide), depth))
    for k in range(1, narrow):
        greet((me, lax.rem(depth + k, narrow)))
    for u in range(ratio):
        @pl.when(jnp.logical_or(ratio * depth + u != me, turned != depth))
        def _():
            greet((ratio * depth + u, turned))
    own_turn = (turned == depth).astype(jnp.int32)
    pl.semaphore_wait(pltpu.get_barrier_semaphore(), wide - 1 + narrow - 1 + ratio - own_turn)

    strand_at = [lax.rem(depth + 1 + k, heads) for k in range(heads)]
    sibling = [head * group + lax.rem(sub + ks, group) for ks in range(group)]

    def ring(k, ka):
        i = strand_at[k]
        other = lax.rem(head + ka, heads) * group + sub
        return remote(
            attended_ref.at[i], gathered.at[head, sub, i],
            ring_send.at[k, ka], ring_recv.at[k, ka], (other, depth)
        )

    def ring_in(k, ka):
        i = strand_at[k]
        source = lax.rem(head + heads - ka, heads)
        return remote(
            attended_ref.at[i], gathered.at[source, sub, i],
            ring_send.at[k, ka], ring_recv.at[k, ka], (source * group + sub, depth)
        )

    def pair(k, ks):
        i = strand_at[k]
        return remote(
            attended_ref.at[i], gathered.at[head, sub, i],
            pair_send.at[k, ks], pair_recv.at[k, ks], (sibling[ks], depth)
        )

    def pair_in(k, ks):
        i = strand_at[k]
        return remote(
            attended_ref.at[i], gathered.at[head, lax.rem(sub + group - ks, group), i],
            pair_send.at[k, ks], pair_recv.at[k, ks], (sibling[ks], depth)
        )

    def hand(k, ka, ks):
        i = strand_at[k]
        held = gathered.at[lax.rem(head + heads - ka, heads), sub, i]
        return remote(held, held, pass_send.at[k, ka, ks], pass_recv.at[k, ka, ks], (sibling[ks], depth))

    def hand_in(k, ka, ks):
        i = strand_at[k]
        held = gathered.at[
            lax.rem(head + heads - ka, heads), lax.rem(sub + group - ks, group), i
        ]
        return remote(held, held, pass_send.at[k, ka, ks], pass_recv.at[k, ka, ks], (sibling[ks], depth))

    for k in range(heads):
        for ka in range(1, heads):
            ring(k, ka).start()
        for ks in range(1, group):
            pair(k, ks).start()
    for k in range(heads):
        gathered[head, sub, strand_at[k]] = attended_ref[strand_at[k]]

    def stage(k):
        for ka in range(1, heads):
            ring_in(k, ka).wait_recv()
            for ks in range(1, group):
                hand(k, ka, ks).start()

    def arrive(k):
        for ks in range(1, group):
            pair_in(k, ks).wait_recv()
            for ka in range(1, heads):
                hand_in(k, ka, ks).wait_recv()

    def project(which):
        route_a, route_b = route_columns(routes_ref[which])
        total = jnp.zeros((block, columns), F32)
        for h in range(heads):
            first = gathered[h, lax.rem(which, group), lax.div(which, group), 0]
            second = gathered[h, lax.rem(which, group), lax.div(which, group), 1]
            nothing = jnp.zeros_like(first)
            padded = jnp.concatenate(
                [
                    jnp.where(route_a == e, first, jnp.where(route_b == e, second, nothing))
                    for e in range(E)
                ],
                axis=1,
            )
            total = total + jnp.dot(
                padded, weight_ref[h * E * H:(h + 1) * E * H, :], preferred_element_type=F32
            )
        return total

    def deep(k):
        to = lax.rem(depth + 1 + k, narrow)
        return remote(parts.at[k], got.at[k], deep_send.at[k], deep_recv.at[k], (me, to))

    one_each = narrow == heads
    if one_each:
        stage(0)
    else:
        for k in range(heads):
            stage(k)
        for k in range(heads):
            arrive(k)
    owned = []
    for k in range(narrow):
        if one_each:
            if k + 1 < heads:
                stage(k + 1)
            arrive(k)
        quarter = lax.rem(depth + 1 + k, narrow)
        for u in range(ratio):
            total = project(quarter * ratio + u)
            if k < narrow - 1:
                parts[k, u] = total.astype(BF16)
            else:
                owned.append(total)
        if k < narrow - 1:
            deep(k).start()
    for k in range(narrow - 1):
        deep(k).wait_recv()
    for u in range(ratio):
        total = owned[u]
        for k in range(narrow - 1):
            total = total + got[k, u].astype(F32)
        mine[u] = total.astype(BF16)

    def turn(u):
        return remote(
            mine.at[u], final.at[lane], turn_send.at[u], turn_recv.at[lane],
            (ratio * depth + u, turned)
        )

    def turn_in(u):
        return remote(
            mine.at[u], final.at[u], turn_send.at[u], turn_recv.at[u],
            (ratio * depth + u, turned)
        )

    for u in range(ratio):
        apart = jnp.logical_or(ratio * depth + u != me, turned != depth)

        @pl.when(apart)
        def _():
            turn(u).start()

        @pl.when(jnp.logical_not(apart))
        def _():
            final[lane] = mine[u]

    for u in range(ratio):
        apart = jnp.logical_or(ratio * depth + u != me, turned != depth)

        @pl.when(apart)
        def _():
            turn_in(u).wait_recv()

        out_ref[:, u * columns:(u + 1) * columns] = final[u]

    for k in range(heads):
        for ka in range(1, heads):
            ring(k, ka).wait_send()
            for ks in range(1, group):
                hand(k, ka, ks).wait_send()
        for ks in range(1, group):
            pair(k, ks).wait_send()
    for k in range(narrow - 1):
        deep(k).wait_send()
    for u in range(ratio):
        @pl.when(jnp.logical_or(ratio * depth + u != me, turned != depth))
        def _():
            turn(u).wait_send()


def on_device(
    wide,
    narrow,
    tokens,
    norm_gain,
    router,
    routes,
    kv_weight,
    query_weight,
    out_weight,
    prefix_cache,
    suffix_lengths,
    prefix_lengths,
):
    block = tokens.shape[0]
    width = router.shape[0]
    heads = kv_weight.shape[0] // (2 * H)
    group = wide // heads
    strands = wide // group
    columns = width // wide
    slots = prefix_cache.shape[0]
    sub = lax.rem(lax.axis_index("wide"), group)
    smem = pl.BlockSpec(memory_space=pltpu.SMEM)
    in_vmem = pl.BlockSpec(memory_space=pltpu.VMEM)
    anywhere = pl.BlockSpec(memory_space=pl.ANY)
    dma = pltpu.SemaphoreType.DMA
    queries, gates, cache, kv, routes_all = pl.pallas_call(
        functools.partial(prepare_kernel, wide, narrow, group),
        out_shape=[
            jax.ShapeDtypeStruct((strands, 2 * block, H), BF16),
            jax.ShapeDtypeStruct((strands, 2 * block, 1), F32),
            jax.ShapeDtypeStruct((wide * slots, 2 * H), BF16),
            jax.ShapeDtypeStruct((group, strands, block, 2 * H), BF16),
            jax.ShapeDtypeStruct((wide, 8, block), jnp.int32),
        ],
        in_specs=[in_vmem] * 4 + [anywhere] * 3,
        out_specs=[in_vmem] * 5,
        scratch_shapes=[
            pltpu.VMEM((narrow,) + tokens.shape, BF16),
            pltpu.VMEM((strands, block, width), BF16),
            pltpu.VMEM((2 * H, width), BF16),
            pltpu.VMEM((E * H, width), BF16),
            pltpu.VMEM((8, block), jnp.int32),
            dma((narrow,)),
            dma((narrow,)),
            dma((wide,)),
            dma((wide,)),
            dma((3, heads, group)),
            dma((3, heads, group)),
            dma((3, heads, group, group)),
            dma((3, heads, group, group)),
            dma((3, group)),
            dma((3, group)),
            dma((3, max(2, heads))),
            dma((3, max(2, heads))),
            dma((heads, group)),
            dma((heads, group)),
            dma((3,)),
        ],
        compiler_params=pltpu.CompilerParams(
            vmem_limit_bytes=56 * 1024 * 1024, collective_id=2, has_side_effects=True
        ),
        name="prepare",
    )(
        tokens,
        norm_gain,
        jnp.transpose(routes),
        jnp.transpose(router),
        kv_weight,
        query_weight,
        prefix_cache,
    )
    attended = pl.pallas_call(
        functools.partial(attend_kernel, group),
        out_shape=jax.ShapeDtypeStruct((strands, 2, block, H), BF16),
        in_specs=[smem] * 3 + [in_vmem] * 4,
        out_specs=in_vmem,
        compiler_params=pltpu.CompilerParams(vmem_limit_bytes=56 * 1024 * 1024),
        name="attend",
    )(
        suffix_lengths,
        prefix_lengths,
        sub[None],
        queries,
        gates,
        cache,
        kv.reshape(wide * block, 2 * H),
    )
    ratio = wide // narrow
    return pl.pallas_call(
        functools.partial(finish_kernel, wide, narrow, group),
        out_shape=jax.ShapeDtypeStruct((block, ratio * columns), BF16),
        in_specs=[in_vmem] * 3,
        out_specs=in_vmem,
        scratch_shapes=[
            pltpu.VMEM((heads, group, strands, 2, block, H), BF16),
            pltpu.VMEM((narrow - 1, ratio, block, columns), BF16),
            pltpu.VMEM((narrow - 1, ratio, block, columns), BF16),
            pltpu.VMEM((ratio, block, columns), BF16),
            pltpu.VMEM((ratio, block, columns), BF16),
            dma((heads, heads)),
            dma((heads, heads)),
            dma((heads, group)),
            dma((heads, group)),
            dma((heads, heads, group)),
            dma((heads, heads, group)),
            dma((narrow,)),
            dma((narrow,)),
            dma((ratio,)),
            dma((ratio,)),
        ],
        compiler_params=pltpu.CompilerParams(
            vmem_limit_bytes=56 * 1024 * 1024, collective_id=1, has_side_effects=True
        ),
        name="finish",
    )(attended, out_weight, routes_all)


def solution(mesh):
    placed = (
        P("wide", "narrow"),
        P(),
        P(),
        P("wide", None),
        P("narrow", "wide"),
        P("narrow", "wide"),
        P("narrow", "wide"),
        P("wide", "narrow"),
        P(),
        P(),
    )
    return jax.shard_map(
        functools.partial(on_device, mesh.shape["wide"], mesh.shape["narrow"]),
        mesh=mesh,
        in_specs=placed,
        out_specs=P("wide", "narrow"),
        check_vma=False,
    )
```

profile of v0, /device:TPU:3, one launch (start us, length us, event | category | flops | bytes accessed | tf_op | source)
XLA Modules:
  0.0 186.5 jit_solution(15036950512071082254)
XLA Ops:
  0.0 93.1 %prepare.1 = (bf16[4,512,128]{2,1,0:T(8,128)(2,1)}, f32[4,512,1]{2,1,0:T(8,128)}, bf16[6144,256]{1,0:T(8,128)(2,1)}, bf16[2,4,256,256]{3,2,1,0:T(8,128)(2,1)}, s32[8,8,256]{2,1,0:T(8,128)}) custom-call(bf16[256,512]{1,0:T(8,128)(2,1)} %tokens_ref.1, bf16[2048]{0:T(1024)(128)(2,1)} %gain_ref.1, s32[2,256]{1,0:T(2,128)} %bitcast.6, bf16[8,2048]{1,0:T(8,128)(2,1)} %bitcast.5, ...), custom_call_target="tpu_custom_call" | custom-call | tf_op jit(solution)/shard_map/prepare/pallas_call | solution.py:718
  93.1 28.1 %attend.1.attended_ref = bf16[4,2,256,128]{3,2,1,0:T(8,128)(2,1)} custom-call(s32[4]{0:T(128)} %suffix_ref.1, s32[4]{0:T(128)} %prefix_ref.1, s32[1]{0:T(128)} %bitcast.sub_ref, bf16[4,512,128]{2,1,0:T(8,128)(2,1)} %get-tuple-element.10.queries_ref, f32[4,512,1]{2,1,0:T(8,128)} %get-tuple-element.11.gates_ref, ...), custom_call_target="tpu_custom_call" | custom-call | tf_op jit(solution)/shard_map/attend/pallas_call | solution.py:764
  121.2 63.6 %finish.1 = bf16[256,512]{1,0:T(8,128)(2,1)} custom-call(bf16[4,2,256,128]{3,2,1,0:T(8,128)(2,1)} %attend.1.attended_ref, bf16[4096,256]{1,0:T(8,128)(2,1)} %weight_ref.1, s32[8,8,256]{2,1,0:T(8,128)} %get-tuple-element.14.routes_ref), custom_call_target="tpu_custom_call" | custom-call | tf_op jit(solution)/shard_map/finish/pallas_call | solution.py:781
  184.8 1.7 copy.12
where the time goes:
time: 186 us
  Pallas kernels  185 us (99%)
    pallas_call x1, Pallas kernels, on_device(): pl.pallas_call(functools.partial(prepare_kernel, wide, narrow, group), ou...  93.1 us
    pallas_call x1, Pallas kernels, on_device(): pl.pallas_call(functools.partial(finish_kernel, wide, narrow, group), out...  63.6 us
    pallas_call x1, Pallas kernels, on_device(): pl.pallas_call(functools.partial(attend_kernel, group), out_shape=jax.Sha...  28.1 us

commit v1 on v0

--- a/solution.py
+++ b/solution.py
@@ -526,20 +526,56 @@
     strand_at = [lax.rem(depth + 1 + k, heads) for k in range(heads)]
     sibling = [head * group + lax.rem(sub + ks, group) for ks in range(group)]
 
+    square = heads == 4 and attended_ref.shape[1] == 2
+    if square:
+        x, y = lax.rem(head, 2), lax.div(head, 2)
+        neighbour = [y * 2 + 1 - x, (1 - y) * 2 + x]
+        origin = [head] + neighbour + [(1 - y) * 2 + 1 - x]
+    else:
+        origin = [lax.rem(head + heads - ka, heads) for ka in range(heads)]
+
+    def near(k, side, piece):
+        i = strand_at[k]
+        return remote(
+            attended_ref.at[i, piece], gathered.at[head, sub, i, piece],
+            ring_send.at[k, side, piece], ring_recv.at[k, side, piece],
+            (neighbour[side] * group + sub, depth)
+        )
+
+    def near_in(k, side, piece):
+        i = strand_at[k]
+        return remote(
+            attended_ref.at[i, piece], gathered.at[neighbour[side], sub, i, piece],
+            ring_send.at[k, side, piece], ring_recv.at[k, side, piece],
+            (neighbour[side] * group + sub, depth)
+        )
+
+    def onward(k, piece):
+        held = gathered.at[neighbour[piece], sub, strand_at[k], piece]
+        return remote(
+            held, held, ring_send.at[k, 2, piece], ring_recv.at[k, 2, piece],
+            (neighbour[1 - piece] * group + sub, depth)
+        )
+
+    def onward_in(k, piece):
+        held = gathered.at[origin[3], sub, strand_at[k], piece]
+        return remote(
+            held, held, ring_send.at[k, 2, piece], ring_recv.at[k, 2, piece],
+            (neighbour[1 - piece] * group + sub, depth)
+        )
+
     def ring(k, ka):
         i = strand_at[k]
-        other = lax.rem(head + ka, heads) * group + sub
-        return remote(
-            attended_ref.at[i], gathered.at[head, sub, i],
-            ring_send.at[k, ka], ring_recv.at[k, ka], (other, depth)
+        return remote(
+            attended_ref.at[i], gathered.at[head, sub, i], ring_send.at[k, 0, ka],
+            ring_recv.at[k, 0, ka], (lax.rem(head + ka, heads) * group + sub, depth)
         )
 
     def ring_in(k, ka):
         i = strand_at[k]
-        source = lax.rem(head + heads - ka, heads)
-        return remote(
-            attended_ref.at[i], gathered.at[source, sub, i],
-            ring_send.at[k, ka], ring_recv.at[k, ka], (source * group + sub, depth)
+        return remote(
+            attended_ref.at[i], gathered.at[origin[ka], sub, i], ring_send.at[k, 0, ka],
+            ring_recv.at[k, 0, ka], (origin[ka] * group + sub, depth)
         )
 
     def pair(k, ks):
@@ -558,29 +594,55 @@
 
     def hand(k, ka, ks):
         i = strand_at[k]
-        held = gathered.at[lax.rem(head + heads - ka, heads), sub, i]
+        held = gathered.at[origin[ka], sub, i]
         return remote(held, held, pass_send.at[k, ka, ks], pass_recv.at[k, ka, ks], (sibling[ks], depth))
 
     def hand_in(k, ka, ks):
         i = strand_at[k]
-        held = gathered.at[
-            lax.rem(head + heads - ka, heads), lax.rem(sub + group - ks, group), i
-        ]
+        held = gathered.at[origin[ka], lax.rem(sub + group - ks, group), i]
         return remote(held, held, pass_send.at[k, ka, ks], pass_recv.at[k, ka, ks], (sibling[ks], depth))
 
-    for k in range(heads):
-        for ka in range(1, heads):
-            ring(k, ka).start()
+    def launch(k):
+        if square:
+            for round in range(2):
+                for side in range(2):
+                    near(k, side, (side + round) % 2).start()
+        else:
+            for ka in range(1, heads):
+                ring(k, ka).start()
         for ks in range(1, group):
             pair(k, ks).start()
+
+    at_first = 2 if square else heads
+    for k in range(at_first):
+        launch(k)
     for k in range(heads):
         gathered[head, sub, strand_at[k]] = attended_ref[strand_at[k]]
 
+    def give(k, ka):
+        for ks in range(1, group):
+            hand(k, ka, ks).start()
+
     def stage(k):
-        for ka in range(1, heads):
-            ring_in(k, ka).wait_recv()
-            for ks in range(1, group):
-                hand(k, ka, ks).start()
+        if square:
+            for piece in range(2):
+                near_in(k, piece, piece).wait_recv()
+                onward(k, piece).start()
+            for side in range(2):
+                near_in(k, side, 1 - side).wait_recv()
+                give(k, 1 + side)
+        else:
+            for ka in range(1, heads):
+                ring_in(k, ka).wait_recv()
+                give(k, ka)
+        if at_first + k < heads:
+            launch(at_first + k)
+
+    def stage_far(k):
+        if square:
+            for piece in range(2):
+                onward_in(k, piece).wait_recv()
+            give(k, 3)
 
     def arrive(k):
         for ks in range(1, group):
@@ -618,10 +680,12 @@
         for k in range(heads):
             stage(k)
         for k in range(heads):
+            stage_far(k)
             arrive(k)
     owned = []
     for k in range(narrow):
         if one_each:
+            stage_far(k)
             if k + 1 < heads:
                 stage(k + 1)
             arrive(k)
@@ -675,8 +739,14 @@
         out_ref[:, u * columns:(u + 1) * columns] = final[u]
 
     for k in range(heads):
+        if square:
+            for piece in range(2):
+                for side in range(2):
+                    near(k, side, piece).wait_send()
+                onward(k, piece).wait_send()
         for ka in range(1, heads):
-            ring(k, ka).wait_send()
+            if not square:
+                ring(k, ka).wait_send()
             for ks in range(1, group):
                 hand(k, ka, ks).wait_send()
         for ks in range(1, group):
@@ -789,8 +859,8 @@
             pltpu.VMEM((narrow - 1, ratio, block, columns), BF16),
             pltpu.VMEM((ratio, block, columns), BF16),
             pltpu.VMEM((ratio, block, columns), BF16),
-            dma((heads, heads)),
-            dma((heads, heads)),
+            dma((heads, 3, max(2, heads))),
+            dma((heads, 3, max(2, heads))),
             dma((heads, group)),
             dma((heads, group)),
             dma((heads, heads, group)),

time: 186 us -> 183 us (0.984); the launches traced: 186 us -> 182 us
  Pallas kernels: 185 us -> 180 us
    pallas_call x1, Pallas kernels: 28.1 us -> 25 us  [on_device(): pl.pallas_call(functools.partial(attend_kernel, group), out_shape=jax.Sha...]
    pallas_call x1, Pallas kernels: 63.6 us -> 61.7 us  [on_device(): pl.pallas_call(functools.partial(finish_kernel, wide, narrow, group), out...]
where the time goes in v1:
time: 183 us; the launch traced here: 182 us
  Pallas kernels  180 us (98%)
    pallas_call x1, Pallas kernels, on_device(): pl.pallas_call(functools.partial(prepare_kernel, wide, narrow, group), ou...  93.1 us
    pallas_call x1, Pallas kernels, on_device(): pl.pallas_call(functools.partial(finish_kernel, wide, narrow, group), out...  61.7 us
    pallas_call x1, Pallas kernels, on_device(): pl.pallas_call(functools.partial(attend_kernel, group), out_shape=jax.Sha...  25 us

profile of v1, /device:TPU:3, one launch (start us, length us, event | category | flops | bytes accessed | tf_op | source)
XLA Modules:
  0.0 181.5 jit_solution(7272127079591597940)
XLA Ops:
  0.0 93.1 %prepare.1 = (bf16[4,512,128]{2,1,0:T(8,128)(2,1)}, f32[4,512,1]{2,1,0:T(8,128)}, bf16[6144,256]{1,0:T(8,128)(2,1)}, bf16[2,4,256,256]{3,2,1,0:T(8,128)(2,1)}, s32[8,8,256]{2,1,0:T(8,128)}) custom-call(bf16[256,512]{1,0:T(8,128)(2,1)} %tokens_ref.1, bf16[2048]{0:T(1024)(128)(2,1)} %gain_ref.1, s32[2,256]{1,0:T(2,128)} %bitcast.6, bf16[8,2048]{1,0:T(8,128)(2,1)} %bitcast.5, ...), custom_call_target="tpu_custom_call" | custom-call | tf_op jit(solution)/shard_map/prepare/pallas_call | solution.py:788
  93.1 25.0 %attend.1.attended_ref = bf16[4,2,256,128]{3,2,1,0:T(8,128)(2,1)} custom-call(s32[4]{0:T(128)} %suffix_ref.1, s32[4]{0:T(128)} %prefix_ref.1, s32[1]{0:T(128)} %bitcast.sub_ref, bf16[4,512,128]{2,1,0:T(8,128)(2,1)} %get-tuple-element.10.queries_ref, f32[4,512,1]{2,1,0:T(8,128)} %get-tuple-element.11.gates_ref, ...), custom_call_target="tpu_custom_call" | custom-call | tf_op jit(solution)/shard_map/attend/pallas_call | solution.py:834
  118.1 61.7 %finish.1 = bf16[256,512]{1,0:T(8,128)(2,1)} custom-call(bf16[4,2,256,128]{3,2,1,0:T(8,128)(2,1)} %attend.1.attended_ref, bf16[4096,256]{1,0:T(8,128)(2,1)} %weight_ref.1, s32[8,8,256]{2,1,0:T(8,128)} %get-tuple-element.14.routes_ref), custom_call_target="tpu_custom_call" | custom-call | tf_op jit(solution)/shard_map/finish/pallas_call | solution.py:851
  179.9 1.7 copy.12
